TPU v7x, 256 devices: a whole 4x4x8 slice. The times are simulated.
256 devices in a mesh: train: 32 (over z, y_lo, core), pre: 8 (over x, y_hi).
Axes of the slice: x: 4, y: 4 (y_hi: 2, y_lo: 2; y = y_hi * 2 + y_lo), z: 8, core: 2. Of those that a mesh axis runs over, the one named last changes fastest.
Arguments:
- gradient: float32 [256, 512, 512], P('pre', 'train'), may hold values from -720 to 720
- assignment: int32 [8, 32], P('pre'), may hold values from 0 to 31, each once within a row
- left_prev: float32 [8, 32, 512, 512], P('pre', 'train'), may hold values from -2 to 3072, as said below
- right_prev: float32 [8, 32, 512, 512], P('pre', 'train'), may hold values from -2 to 3072, as said below
Outputs:
- update: float32 [256, 512, 512], P('pre', 'train')
- left_root: float32 [256, 512, 512], P('pre', 'train')
- right_root: float32 [256, 512, 512], P('pre', 'train')
- left_stat: float32 [8, 32, 512, 512], P('pre', 'train')
- right_stat: float32 [8, 32, 512, 512], P('pre', 'train')
Inputs may be any that keep to these rules, and one draw needn't show every extreme that they name: `assignment`: each row lists every block number of its group once. `left_prev`: each block is symmetric and positive definite. `right_prev`: each block is symmetric and positive definite.
All inputs are finite; a program needn't handle non-finite values.
Results may differ from a plain program's by a relative error of at most 0.0095.
The roundings to bfloat16 on the way count: a program that leaves them out, or rounds other values in their place, can miss the bound.
Values sent between devices are 32-bit elements; how exact they have to be, the bound alone decides.
A program may use at most 64 MiB of HBM per device.

v0:
```python
import jax
import jax.numpy as jnp
from jax import lax
from jax.sharding import PartitionSpec as P

ITERS = 3


decay_rate = 0.95
highest = lax.Precision.HIGHEST


def full_product(left, right):
    return jnp.dot(left, right, precision=highest, preferred_element_type=jnp.float32)


def half_product(left, right):
    return jnp.dot(left, right, preferred_element_type=jnp.float32)


def inverse_root(statistic):
    identity = jnp.eye(statistic.shape[0], dtype=jnp.float32)
    start_scale = 2.5 / jnp.sqrt(jnp.sum(statistic * statistic))
    iterate = start_scale * statistic
    root_part = jnp.sqrt(jnp.sqrt(start_scale)) * identity
    for sweep in range(ITERS):
        factor = (1.25 * identity - 0.25 * iterate).astype(jnp.bfloat16)
        square = half_product(factor, factor).astype(jnp.bfloat16)
        fourth = half_product(square, square).astype(jnp.bfloat16)
        iterate = half_product(fourth, iterate.astype(jnp.bfloat16))
        root_part = half_product(root_part.astype(jnp.bfloat16), factor)
    return root_part


def left_phase(pieces):
    grad_block, old_stat = pieces
    new_stat = decay_rate * old_stat + (1.0 - decay_rate) * full_product(grad_block, grad_block.T)
    return (new_stat, inverse_root(new_stat))


def right_phase(pieces):
    grad_block, old_stat, left_factor = pieces
    new_stat = decay_rate * old_stat + (1.0 - decay_rate) * full_product(grad_block.T, grad_block)
    right_factor = inverse_root(new_stat)
    precond = full_product(left_factor, full_product(grad_block, right_factor))
    return (new_stat, right_factor, precond)


def shards(gradient, assignment, left_prev, right_prev):
    trainers = lax.axis_size("train")
    block_count, row_count, block_width = gradient.shape
    slot_count = block_count // trainers
    block_order = assignment[0]
    outgoing = jnp.take(gradient, block_order, axis=0).reshape(
        trainers, slot_count, row_count, block_width
    )
    arrived = lax.all_to_all(outgoing, "train", split_axis=0, concat_axis=2, tiled=True)
    owned = arrived.reshape(slot_count, row_count * trainers, block_width)

    def split_rows(values):
        return values.reshape(slot_count, trainers, row_count, block_width)

    def to_blocks(values):
        in_slots = values.reshape(block_count, row_count, block_width)
        return jnp.zeros_like(in_slots).at[block_order].set(in_slots)

    left_new, left_factor = lax.map(left_phase, (owned, left_prev[0]))
    right_new, right_factor, precond = lax.map(right_phase, (owned, right_prev[0], left_factor))
    prec_home, left_home, right_home = (
        lax.all_to_all(split_rows(precond), "train", split_axis=1, concat_axis=0, tiled=True),
        lax.all_to_all(split_rows(left_factor), "train", split_axis=1, concat_axis=0, tiled=True),
        lax.all_to_all(split_rows(right_factor), "train", split_axis=1, concat_axis=0, tiled=True),
    )
    prec_local = jnp.sum(precond * precond)
    grad_total, prec_total = lax.psum((jnp.sum(owned * owned), prec_local), ("train", "pre"))
    graft = jnp.sqrt(grad_total / (prec_total + 1e-06))
    update = to_blocks(prec_home) * graft
    return (update, to_blocks(left_home), to_blocks(right_home), left_new[None], right_new[None])


def solution(mesh):
    return jax.shard_map(
        shards,
        mesh=mesh,
        in_specs=(
            P("pre", "train", None),
            P("pre", None),
            P("pre", "train", None, None),
            P("pre", "train", None, None),
        ),
        out_specs=(
            P("pre", "train", None),
            P("pre", "train", None),
            P("pre", "train", None),
            P("pre", "train", None, None),
            P("pre", "train", None, None),
        ),
        check_vma=False,
    )
```

profile of v0, /device:TPU:1, one launch (start us, length us, event | category | flops | bytes accessed | tf_op | source)
XLA Modules:
  0.0 254.2 jit_solution(10883023169728368146)
XLA Ops:
  0.7 0.8 fusion.32
  1.4 0.5 copy-done
  1.9 0.6 gather_fusion
  2.7 39.2 %all_to_all.16 = f32[32,1,16,512]{3,2,1,0:T(8,128)S(1)} all-to-all(f32[32,1,16,512]{3,2,1,0:T(8,128)S(1)} %fusion.12), channel_id=1, replica_groups=mesh['train'=32,'pre'=8] {'train'}, dimensions={0} | all-to-all | bytes 2097152 | tf_op jit(solution)/shard_map/all_to_all | solution.py:57
  41.9 3.6 %multiply_reduce_fusion.2 = (f32[]{:T(128)}, f32[512,512]{1,0:T(8,128)S(1)}) fusion(f32[32,1,16,512]{3,2,1,0:T(8,128)S(1)} %all_to_all.16, f32[1,1,512,512]{3,2,1,0:T(8,128)S(1)} %copy-done.8), kind=kOutput, calls=%fused_computation.44 | convolution fusion | flops 1611923456 | bytes 3145732 | tf_op jit(solution)/shard_map/while/body/eval_jaxpr/dot_general | solution.py:14
  46.2 1.9 convolution_convert_fusion.3
  48.1 2.5 fusion.15
  50.6 4.5 %convolution_convert_fusion = bf16[512,512]{1,0:T(8,128)(2,1)} fusion(f32[512,512]{1,0:T(8,128)} %fusion.15), kind=kOutput, calls=%fused_computation.17 | convolution fusion | flops 538705920 | bytes 1572864 | tf_op jit(solution)/shard_map/while/body/eval_jaxpr/dot_general | solution.py:18
  55.1 2.6 %fusion.4 = bf16[512,512]{1,0:T(8,128)(2,1)} fusion(bf16[512,512]{1,0:T(8,128)(2,1)} %convolution_convert_fusion, f32[512,512]{1,0:T(8,128)} %fusion.15), kind=kOutput, calls=%fused_computation.30 | convolution fusion | flops 270008320 | bytes 2097152 | tf_op jit(solution)/shard_map/while/body/eval_jaxpr/dot_general | solution.py:18
  57.7 1.3 convolution_convert_fusion.5
  59.0 2.3 fusion.6
  61.3 1.0 copy-done.2
  62.3 2.8 %fusion.65 = f32[512,512]{1,0:T(8,128)} fusion(f32[512,512]{1,0:T(8,128)S(1)} %bitcast.56, f32[512,512]{1,0:T(8,128)S(1)} %fusion.6), kind=kOutput, calls=%fused_computation.80 | convolution fusion | flops 1610612736 | bytes 3145728 | tf_op jit(solution)/shard_map/while/body/eval_jaxpr/dot_general | solution.py:14
  65.1 2.6 %multiply_reduce_fusion.3 = (f32[]{:T(128)}, f32[512,512]{1,0:T(8,128)S(1)}) fusion(f32[512,512]{1,0:T(8,128)S(1)} %bitcast.57, f32[1,1,512,512]{3,2,1,0:T(8,128)S(1)} %copy-done.6), kind=kOutput, calls=%fused_computation.46 | convolution fusion | flops 1611923456 | bytes 3145732 | tf_op jit(solution)/shard_map/while/body/eval_jaxpr/dot_general | solution.py:14
  68.5 1.9 convolution_convert_fusion.9
  70.4 2.5 fusion.14
  72.8 4.6 %convolution_convert_fusion.6 = bf16[512,512]{1,0:T(8,128)(2,1)} fusion(f32[512,512]{1,0:T(8,128)} %fusion.14), kind=kOutput, calls=%fused_computation.23 | convolution fusion | flops 538705920 | bytes 1572864 | tf_op jit(solution)/shard_map/while/body/eval_jaxpr/dot_general | solution.py:18
  77.5 2.6 %fusion.3 = bf16[512,512]{1,0:T(8,128)(2,1)} fusion(bf16[512,512]{1,0:T(8,128)(2,1)} %convolution_convert_fusion.6, f32[512,512]{1,0:T(8,128)} %fusion.14), kind=kOutput, calls=%fused_computation.29 | convolution fusion | flops 270008320 | bytes 2097152 | tf_op jit(solution)/shard_map/while/body/eval_jaxpr/dot_general | solution.py:18
  80.2 1.3 convolution_convert_fusion.11
  81.5 3.3 %fusion.5 = f32[512,512]{1,0:T(8,128)} fusion(bf16[512,512]{1,0:T(8,128)(2,1)} %fusion.3, bf16[512,512]{1,0:T(8,128)(2,1)} %convolution_convert_fusion.11, f32[512,512]{1,0:T(8,128)} %fusion.14), kind=kOutput, calls=%fused_computation.31 | convolution fusion | flops 538443776 | bytes 3145728 | tf_op jit(solution)/shard_map/while/body/eval_jaxpr/dot_general | solution.py:18
  84.8 3.8 %multiply_reduce_fusion = (f32[]{:T(128)}, f32[512,512]{1,0:T(8,128)S(1)}) fusion(f32[512,512]{1,0:T(8,128)} %fusion.5, f32[512,512]{1,0:T(8,128)S(1)} %copy-done.4), kind=kOutput, calls=%fused_computation.41 | convolution fusion | flops 1611137024 | bytes 3145732 | tf_op jit(solution)/shard_map/while/body/eval_jaxpr/dot_general | solution.py:14
  88.6 32.8 %all_to_all.17 = f32[1,32,16,512]{3,2,0,1:T(8,128)} all-to-all(f32[1,32,16,512]{3,2,0,1:T(8,128)S(1)} %bitcast.63), channel_id=1, replica_groups=mesh['train'=32,'pre'=8] {'train'}, dimensions={1} | all-to-all | bytes 2097152 | tf_op jit(solution)/shard_map/all_to_all | solution.py:70
  121.4 32.9 %all_to_all.18 = f32[1,32,16,512]{3,2,0,1:T(8,128)} all-to-all(f32[1,32,16,512]{3,2,0,1:T(8,128)S(1)} %bitcast.59), channel_id=1, replica_groups=mesh['train'=32,'pre'=8] {'train'}, dimensions={1} | all-to-all | bytes 2097152 | tf_op jit(solution)/shard_map/all_to_all | solution.py:72
  154.3 5.0 %all-to-all-start.2 = ((f32[1,32,16,512]{3,2,0,1:T(8,128)}), f32[1,32,16,512]{3,2,0,1:T(8,128)S(1)}, u32[]{:S(2)}, u32[]{:S(2)}) async-start(f32[1,32,16,512]{3,2,0,1:T(8,128)} %bitcast.14), calls=%async_computation.2 | async-start | bytes 2097152 | tf_op jit(solution)/shard_map/all_to_all | solution.py:71
  159.3 0.9 multiply_reduce_fusion.1
  160.2 78.8 %all-reduce = (f32[]{:T(128)}, f32[]{:T(128)}) all-reduce(f32[]{:T(128)} %multiply_reduce_fusion.1, f32[]{:T(128)} %get-tuple-element.40), channel_id=1, replica_groups=mesh['train'=32,'pre'=8] {'train','pre'}, use_global_device_ids=true, to_apply=%region_4.5 | all-reduce | flops 2 | bytes 16 | tf_op jit(solution)/shard_map/psum | solution.py:75
  240.4 3.6 %scatter_fusion = f32[32,16,512]{2,1,0:T(8,128)S(1)} fusion(f32[32,16,512]{2,1,0:T(8,128)S(1)} %broadcast.84.clone, s32[32]{0:T(128)S(1)} %fusion.32, f32[32,16,512]{2,1,0:T(8,128)} %bitcast.62), kind=kCustom, calls=%fused_computation.1 | custom fusion | bytes 3145856 | tf_op jit(solution)/shard_map/scatter | solution.py:65
  244.0 1.1 broadcast.84.clone.2
  245.1 5.2 %scatter_fusion.2 = f32[32,16,512]{2,1,0:T(8,128)} fusion(f32[32,16,512]{2,1,0:T(8,128)} %broadcast.84.clone.2, s32[32]{0:T(128)S(1)} %fusion.32, f32[32,16,512]{2,1,0:T(8,128)} %bitcast.61), kind=kCustom, calls=%fused_computation.3 | custom fusion | bytes 3145856 | tf_op jit(solution)/shard_map/scatter | solution.py:65
  250.4 1.1 broadcast_multiply_fusion
  251.6 1.6 scatter_fusion.1
  253.2 1.0 copy-done.5
  (23 shorter events, 0.4 us)
Async XLA Ops:
  0.6 1.3 copy-start
  0.6 0.8 copy-start.9
  2.7 39.2 %copy-start.8 = (f32[1,1,512,512]{3,2,1,0:T(8,128)S(1)}, f32[1,1,512,512]{3,2,1,0:T(8,128)}, u32[]{:S(2)}) copy-start(f32[1,1,512,512]{3,2,1,0:T(8,128)} %param.7) | copy-start | bytes 3145732
  45.5 12.2 %copy-start.7 = (f32[512,512]{1,0:T(8,128)}, f32[512,512]{1,0:T(8,128)S(1)}, u32[]{:S(2)}) copy-start(f32[512,512]{1,0:T(8,128)S(1)} %get-tuple-element.39) | copy-start | bytes 3145732
  61.3 1.0 copy-start.2
  62.3 2.8 %copy-start.6 = (f32[1,1,512,512]{3,2,1,0:T(8,128)S(1)}, f32[1,1,512,512]{3,2,1,0:T(8,128)}, u32[]{:S(2)}) copy-start(f32[1,1,512,512]{3,2,1,0:T(8,128)} %param.6) | copy-start | bytes 3145732
  67.7 12.4 %copy-start.1 = (f32[512,512]{1,0:T(8,128)}, f32[512,512]{1,0:T(8,128)S(1)}, u32[]{:S(2)}) copy-start(f32[512,512]{1,0:T(8,128)S(1)} %get-tuple-element.37) | copy-start | bytes 3145732
  81.5 3.3 %copy-start.4 = (f32[512,512]{1,0:T(8,128)S(1)}, f32[512,512]{1,0:T(8,128)}, u32[]{:S(2)}) copy-start(f32[512,512]{1,0:T(8,128)} %fusion.65) | copy-start | bytes 3145732
  88.6 32.8 %copy-start.3 = (f32[512,512]{1,0:T(8,128)S(1)}, f32[512,512]{1,0:T(8,128)}, u32[]{:S(2)}) copy-start(f32[512,512]{1,0:T(8,128)} %copy-done.2) | copy-start | bytes 3145732
  154.3 97.2 %all-to-all-start.2 = ((f32[1,32,16,512]{3,2,0,1:T(8,128)}), f32[1,32,16,512]{3,2,0,1:T(8,128)S(1)}, u32[]{:S(2)}, u32[]{:S(2)}) async-start(f32[1,32,16,512]{3,2,0,1:T(8,128)} %bitcast.14), calls=%async_computation.2 | async-start | bytes 2097152 | tf_op jit(solution)/shard_map/all_to_all | solution.py:71
  253.2 1.0 copy-start.5
where the time goes:
time: 255 us; the launch traced here: 254 us
  blocking collectives  184 us (72%)
  matrix products  44.1 us (17%)
  local copies, waits for them, and re-layouts  14.8 us (6%)
  starting transfers between devices  4.99 us (2%)
  between operations  3.7 us (1%)
  other arithmetic  2.88 us (1%)
    psum x1, blocking collectives, shards(): lax.psum((jnp.sum(owned * owned), prec_local), ('train', 'pre'))  78.8 us
    all_to_all x1, blocking collectives, shards(): lax.all_to_all(outgoing, 'train', split_axis=0, concat_axis=2, tiled=True)  39.2 us
    all_to_all x1, blocking collectives, shards(): lax.all_to_all(split_rows(right_factor), 'train', split_axis=1, concat_ax...  32.9 us
    all_to_all x1, blocking collectives, shards(): lax.all_to_all(split_rows(precond), 'train', split_axis=1, concat_axis=0,...  32.8 us
    dot_general x12, matrix products, half_product(): return jnp.dot(left, right, preferred_element_type=jnp.float32)  31.3 us
    dot_general x4, matrix products, full_product(): jnp.dot(left, right, precision=highest, preferred_element_type=jnp.float32)  12.9 us
    scatter x3, local copies, waits for them, and re-layouts, to_blocks(): return jnp.zeros_like(in_slots).at[block_order].set(in_slots)  10.4 us
  transfers between devices with their start and end apart: 1, of which 0 were waited for; matrix products, arithmetic and copies ran while one was open for 5% of the time, Pallas kernels for 0%

commit v1 on v0

v1 whole, which is shorter than its diff:
```python
import jax
import jax.numpy as jnp
from jax import lax
from jax.experimental import pallas as pl
from jax.experimental.pallas import tpu as pltpu
from jax.sharding import PartitionSpec as P

MESH = pl.DeviceIdType.MESH
DECAY = 0.95
ITERS = 3
RINGS = 8
SUBS = 4


def split(values):
    high = values.astype(jnp.bfloat16)
    low = (values - high.astype(jnp.float32)).astype(jnp.bfloat16)
    return high, low


def dot(left, right):
    return jnp.dot(left, right, preferred_element_type=jnp.float32)


def dot_t(left, right):
    return lax.dot_general(
        left, right, (((1,), (1,)), ((), ())), preferred_element_type=jnp.float32
    )


def total(values):
    return jnp.sum(jnp.sum(values, axis=0, keepdims=True), axis=1, keepdims=True)


def halves(width):
    return [slice(start, start + width // 2) for start in (0, width // 2)]


def product(left, right, finish):
    for part in halves(right.shape[1]):
        finish(part, dot(left[...], right[:, part]))


def product_full(left_high, left_low, right_high, right_low, finish):
    for part in halves(right_high.shape[1]):
        cross = dot(left_high[...], right_low[:, part]) + dot(left_low[...], right_high[:, part])
        finish(part, dot(left_high[...], right_high[:, part]) + cross)


def keep(target):
    def finish(part, values):
        target[:, part] = values.astype(target.dtype)

    return finish


def put_factor(factor, part, iterate):
    for rows in halves(factor.shape[0]):
        values = -0.25 * iterate[rows]
        if rows == part:
            shape = values.shape
            diagonal = lax.broadcasted_iota(jnp.int32, shape, 0) == lax.broadcasted_iota(
                jnp.int32, shape, 1
            )
            values = jnp.where(diagonal, 1.25 + values, values)
        factor[rows, part] = values.astype(jnp.bfloat16)


def inverse_root(stat, squares, factor, square, fourth, iterate, root, finish):
    scale = 2.5 / jnp.sqrt(squares)
    start = jnp.sqrt(jnp.sqrt(scale)).astype(jnp.bfloat16).astype(jnp.float32)
    for part in halves(stat.shape[1]):
        values = scale * stat[:, part]
        iterate[0, :, part] = values.astype(jnp.bfloat16)
        put_factor(factor.at[0], part, values)
        root[0, :, part] = (start * factor[0, :, part].astype(jnp.float32)).astype(jnp.bfloat16)

    def advance(now, last):
        def finish_iterate(part, values):
            if not last:
                iterate[now + 1, :, part] = values.astype(jnp.bfloat16)
            put_factor(factor.at[now + 1], part, values)

        product(factor.at[now], factor.at[now], keep(square))
        product(square, square, keep(fourth))
        product(fourth, iterate.at[now], finish_iterate)

    advance(0, False)
    product(root.at[0], factor.at[1], keep(root.at[1]))
    advance(1, True)
    product(root.at[1], factor.at[2], finish)


def body(
    order_hbm, grad_hbm, left_prev, right_prev,
    precond_in, left_root_hbm, right_root_hbm, left_stat_hbm, right_stat_hbm, norm_hbm,
    grad, outgoing, owned, left_old, right_old, left_new, right_new,
    left, right, precond, left_in, right_in, ready,
    high, low, other_high, other_low, factor, square, fourth, iterate, root,
    norm, norm_group, norm_all, norm_pre, norm_train, order, place,
    in_sems, out_sems, send_sems, recv_grad, recv_sems, norm_send, norm_recv,
):
    me, group = lax.axis_index("train"), lax.axis_index("pre")
    n, groups = lax.axis_size("train"), lax.axis_size("pre")
    blocks, rows, width = grad.shape
    plane, y_at, core_at = me // SUBS, (me // 2) % 2, me % 2

    barrier = pltpu.get_barrier_semaphore()

    load_left = pltpu.make_async_copy(left_prev, left_old, in_sems.at[1])
    load_right = pltpu.make_async_copy(right_prev, right_old, in_sems.at[2])
    load_order = pltpu.make_async_copy(order_hbm, order, in_sems.at[3])
    load_order.start()
    load_grad = copy_in_parts(grad_hbm, grad, in_sems.at[pl.ds(4, 4)])
    load_left.start()
    load_right.start()
    def greet_train(k, _):
        pl.semaphore_signal(
            barrier, inc=1, device_id={"train": (me + k) % n}, device_id_type=MESH
        )
        return 0

    def greet_pre(k, _):
        pl.semaphore_signal(
            barrier, inc=1, device_id={"pre": (group + k) % groups}, device_id_type=MESH
        )
        return 0

    lax.fori_loop(1, n, greet_train, 0)

    @pl.when(me == 0)
    def _():
        lax.fori_loop(1, groups, greet_pre, 0)

    load_order.wait()
    for load in load_grad:
        load.wait()

    def pick(slot, _):
        outgoing[slot] = grad[order[0, slot]]
        return 0

    lax.fori_loop(0, n, pick, 0)
    pl.semaphore_wait(barrier, n - 1 + jnp.where(me == 0, groups - 1, 0))

    def offset(half, k, core):
        step = half * (RINGS // 2) + k % (RINGS // 2)
        way = (2 * (step % 2) - 1) * (1 - 2 * core)
        return (RINGS - step) // 2 * way, (step + k // (RINGS // 2) + 2) % SUBS

    def device_at(dz, sub):
        z = (plane + dz + RINGS) % RINGS
        return (z * 2 + (y_at + sub // 2) % 2) * 2 + (core_at + sub) % 2

    def push(source, target, send_sem, recv_sem, other):
        pltpu.make_async_remote_copy(
            src_ref=source,
            dst_ref=target,
            send_sem=send_sem,
            recv_sem=recv_sem,
            device_id={"train": other},
            device_id_type=MESH,
        ).start()

    def send_grad(core, half, some=None):
        def send(j, _):
            if some is None:
                step, across = half * (RINGS // 2) + j // 2, (j + 1) % 2
            else:
                step = half * (RINGS // 2) + j
                across = (plane + (RINGS - step) // 2 + y_at + some) % 2
            sub = 2 * across + (core_at + core) % 2
            slot = (sub - step + 10) % SUBS * SUBS + step % (RINGS // 2)
            dz, _ = offset(half, slot, core_at)
            other = device_at(dz, sub)
            at = half * (n // 2) + slot
            push(outgoing.at[other], owned.at[at], send_sems.at[0], recv_grad.at[half], other)
            return 0

        own = core_at == core
        if some is not None:
            own &= (plane + y_at) % 2 == some
        count = RINGS if some is None else RINGS // 2
        lax.fori_loop(0, count - half * jnp.where(own, 1, 0), send, 0)

    def send_half(source, target, which, half):
        def send(k, _):
            other = device_at(*offset(half, k, core_at))
            push(source.at[other], target.at[me], send_sems.at[which], recv_sems.at[which], other)
            return 0

        lax.fori_loop(0, n // 2 - half, send, 0)

    def send_all(source, target, which):
        send_half(source, target, which, 0)
        send_half(source, target, which, 1)

    def wait_bytes(ref, sem, count=n - 1):
        some = ref.at[pl.ds(0, count)]
        pltpu.make_async_copy(some, some, sem).wait()

    for core, some in ((0, None), (1, 0), (1, 1)):
        for half in range(2):
            send_grad(core, half, some)
    owned[n - 1] = outgoing[me]

    def invert(block, _):
        def look(slot, found):
            return jnp.where(order[0, slot] == block, slot, found)

        place[block] = lax.fori_loop(0, n, look, 0)
        return 0

    lax.fori_loop(0, blocks, invert, 0)
    grad_sum = total(jnp.sum(grad[...] * grad[...], axis=0))

    def whole(values, count=n):
        return values.reshape(count * rows, width)

    def gram_of(half):
        count = n // 2
        some_high, some_low = split(whole(owned[half * count : (half + 1) * count], count))
        turned_high, turned_low = some_high.T, some_low.T
        for part in halves(width):
            cross = dot(turned_high, some_low[:, part]) + dot(turned_low, some_high[:, part])
            yield part, dot(turned_high, some_high[:, part]) + cross

    def keep_stat(stat, parts):
        squares = jnp.zeros((1, width // 2), jnp.float32)
        for part, values in parts:
            stat[:, part] = values
            squares += jnp.sum(values * values, axis=0, keepdims=True)
        return jnp.sum(squares, axis=1, keepdims=True)

    def put_root(stat, squares, target):
        def finish(part, values):
            target[:, :, part] = values.reshape(n, rows, width // 2)

        inverse_root(stat, squares, factor, square, fourth, iterate, root, finish)

    load_right.wait()
    wait_bytes(owned, recv_grad.at[0], n // 2)
    for part, gram in gram_of(0):
        right_new[:, part] = DECAY * right_old[:, part] + (1.0 - DECAY) * gram
    wait_bytes(owned.at[pl.ds(n // 2, n // 2)], recv_grad.at[1], n // 2 - 1)
    squares = keep_stat(
        right_new,
        [
            (part, right_new[:, part] + (1.0 - DECAY) * gram)
            for part, gram in gram_of(1)
        ],
    )
    store_right_stat = pltpu.make_async_copy(right_new, right_stat_hbm, out_sems.at[1])
    store_right_stat.start()
    put_root(right_new, squares, right)
    send_all(right, right_in, 1)
    right_in[me] = right[me]

    def place_rows(k, _):
        half, slot = k // (n // 2), k % (n // 2)
        _, sub = offset(half, slot, 0)
        dz, _ = offset(half, slot, (core_at + sub) % 2)
        at = pl.ds(pl.multiple_of(device_at(-dz, sub) * rows, rows), rows)
        high[at], low[at] = split(owned[k])
        return 0

    lax.fori_loop(0, n, place_rows, 0)
    load_left.wait()
    parts = []
    for part in halves(width):
        gram = dot_t(high[...], high[part]) + (
            dot_t(high[...], low[part]) + dot_t(low[...], high[part])
        )
        parts.append((part, DECAY * left_old[:, part] + (1.0 - DECAY) * gram))
    squares = keep_stat(left_new, parts)
    store_left_stat = pltpu.make_async_copy(left_new, left_stat_hbm, out_sems.at[0])
    store_left_stat.start()
    put_root(left_new, squares, left)
    left_in[me] = left[me]

    def keep_split(part, values):
        right_old[:, part] = values

    other_high[...], other_low[...] = split(whole(right[...]))
    product_full(high, low, other_high, other_low, keep_split)
    high[...], low[...] = split(right_old[...])
    other_high[...], other_low[...] = split(whole(left[...]))

    def keep_precond(part, values):
        precond[:, :, part] = values.reshape(n, rows, width // 2)

    product_full(other_high, other_low, high, low, keep_precond)
    prec_sum = total(jnp.sum(precond[...] * precond[...], axis=0))
    upper = lax.broadcasted_iota(jnp.int32, norm.shape, 0) < 4
    norm[...] = jnp.where(upper, grad_sum, prec_sum)

    def share(source, target, which, device):
        pltpu.make_async_remote_copy(
            src_ref=source,
            dst_ref=target,
            send_sem=norm_send.at[which],
            recv_sem=norm_recv.at[which],
            device_id=device,
            device_id_type=MESH,
        ).start()

    def share_pre(k, _):
        share(norm_group, norm_pre.at[group], 1, {"pre": (group + k) % groups})
        return 0

    def share_train(k, _):
        share(norm_all, norm_all, 2, {"train": k})
        return 0

    @pl.when(me != 0)
    def _():
        share(norm, norm_train.at[me], 0, {"train": 0})

    send_all(left, left_in, 2)

    @pl.when(me == 0)
    def _():
        norm_train[0] = norm[...]
        wait_bytes(norm_train, norm_recv.at[0])
        norm_group[...] = jnp.sum(norm_train[...], axis=0)
        lax.fori_loop(1, groups, share_pre, 0)
        norm_pre[group] = norm_group[...]

    send_half(precond, precond_in, 3, 0)

    @pl.when(me == 0)
    def _():
        wait_bytes(norm_pre, norm_recv.at[1], groups - 1)
        wait_bytes(norm_pre, norm_send.at[1], groups - 1)
        norm_all[...] = jnp.sum(norm_pre[...], axis=0)
        lax.fori_loop(1, n, share_train, 0)

    send_half(precond, precond_in, 3, 1)
    keep_own = pltpu.make_async_copy(precond.at[me], precond_in.at[me], out_sems.at[4])
    keep_own.start()

    def to_blocks(source, target, which):
        def move(block, _):
            ready[which, block] = source[place[block]]
            return 0

        lax.fori_loop(0, blocks, move, 0)
        store = pltpu.make_async_copy(ready.at[which], target, out_sems.at[2 + which])
        store.start()
        return store

    wait_bytes(right_in, recv_sems.at[1])
    store_right = to_blocks(right_in, right_root_hbm, 1)
    wait_bytes(left_in, recv_sems.at[2])
    store_left = to_blocks(left_in, left_root_hbm, 0)

    @pl.when(me != 0)
    def _():
        pltpu.make_async_copy(norm, norm, norm_send.at[0]).wait()
        pltpu.make_async_copy(norm_all, norm_all, norm_recv.at[2]).wait()

    @pl.when(me == 0)
    def _():
        wait_bytes(norm_train, norm_send.at[2])

    store_norm = pltpu.make_async_copy(norm_all, norm_hbm, out_sems.at[5])
    store_norm.start()
    wait_bytes(owned, send_sems.at[0])
    wait_bytes(right, send_sems.at[1])
    wait_bytes(left, send_sems.at[2])
    wait_bytes(precond, send_sems.at[3])
    store_left_stat.wait()
    store_right_stat.wait()
    store_left.wait()
    store_right.wait()
    store_norm.wait()
    keep_own.wait()
    wait_bytes(precond_in, recv_sems.at[3])


def in_hbm(value):
    return pltpu.with_memory_space_constraint(value, pltpu.HBM)


def copy_in_parts(source, target, sems):
    count = source.shape[0] // 4
    parts = [pl.ds(part * count, count) for part in range(4)]
    copies = [
        pltpu.make_async_copy(source.at[at], target.at[at], sems.at[part])
        for part, at in enumerate(parts)
    ]
    for copy in copies:
        copy.start()
    return copies


def deliver(
    order_hbm, precond_hbm, left, right, left_stat, right_stat, norm_hbm,
    update, left_out, right_out, left_stat_out, right_stat_out,
    precond, norm, order, in_sems, out_sems,
):
    blocks = precond.shape[0]
    load_order = pltpu.make_async_copy(order_hbm, order, in_sems.at[4])
    load_norm = pltpu.make_async_copy(norm_hbm, norm, in_sems.at[5])
    load_order.start()
    load_norm.start()
    loads = copy_in_parts(precond_hbm, precond, in_sems)
    pairs = ((left, left_out), (right, right_out), (left_stat, left_stat_out), (right_stat, right_stat_out))
    stores = []
    for i, (source, target) in enumerate(pairs):
        stores += copy_in_parts(source, target, out_sems.at[pl.ds(4 * i, 4)])
    load_order.wait()
    load_norm.wait()
    graft = jnp.sqrt(norm[0:1, 0:1] / (norm[4:5, 0:1] + 1e-6))

    def scale(slot, _):
        precond[slot] = precond[slot] * graft
        pltpu.make_async_copy(
            precond.at[slot], update.at[order[0, slot]], out_sems.at[16]
        ).start()
        return 0

    for part, load in enumerate(loads):
        load.wait()
        lax.fori_loop(part * (blocks // 4), (part + 1) * (blocks // 4), scale, 0)
    for store in stores:
        store.wait()
    pltpu.make_async_copy(precond, update, out_sems.at[16]).wait()


def shards(gradient, assignment, left_prev, right_prev):
    n, groups = lax.axis_size("train"), lax.axis_size("pre")
    blocks, rows, width = gradient.shape
    pieces = jax.ShapeDtypeStruct((blocks, rows, width), jnp.float32)
    square = jax.ShapeDtypeStruct((width, width), jnp.float32)
    any_space = pl.BlockSpec(memory_space=pl.ANY)
    pieces_vmem = pltpu.VMEM(pieces.shape, jnp.float32)
    square_vmem = pltpu.VMEM(square.shape, jnp.float32)
    square_half = pltpu.VMEM(square.shape, jnp.bfloat16)
    results = (pieces, pieces, pieces, square, square)
    made = pl.pallas_call(
        body,
        out_shape=results + (jax.ShapeDtypeStruct((8, 128), jnp.float32),),
        in_specs=[pl.BlockSpec(memory_space=pltpu.HBM)] * 4,
        out_specs=(any_space,) * 6,
        scratch_shapes=[pieces_vmem] * 3
        + [square_vmem] * 4
        + [pieces_vmem] * 5
        + [
            pltpu.VMEM((2,) + pieces.shape, jnp.float32),
        ]
        + [square_half] * 4
        + [
            pltpu.VMEM((ITERS,) + square.shape, jnp.bfloat16),
            square_half,
            square_half,
            pltpu.VMEM((ITERS - 1,) + square.shape, jnp.bfloat16),
            pltpu.VMEM((ITERS - 1,) + square.shape, jnp.bfloat16),
            pltpu.VMEM((8, 128), jnp.float32),
            pltpu.VMEM((8, 128), jnp.float32),
            pltpu.VMEM((8, 128), jnp.float32),
            pltpu.VMEM((groups, 8, 128), jnp.float32),
            pltpu.VMEM((n, 8, 128), jnp.float32),
            pltpu.SMEM((1, blocks), jnp.int32),
            pltpu.SMEM((blocks,), jnp.int32),
            pltpu.SemaphoreType.DMA((8,)),
            pltpu.SemaphoreType.DMA((6,)),
            pltpu.SemaphoreType.DMA((4,)),
            pltpu.SemaphoreType.DMA((2,)),
            pltpu.SemaphoreType.DMA((4,)),
            pltpu.SemaphoreType.DMA((3,)),
            pltpu.SemaphoreType.DMA((3,)),
        ],
        compiler_params=pltpu.CompilerParams(
            collective_id=0, has_side_effects=True, vmem_limit_bytes=48 * 2**20
        ),
        cost_estimate=pl.CostEstimate(
            flops=2 * 28 * width**3, bytes_accessed=32 * width**2, transcendentals=0
        ),
        name="shampoo",
    )(*(in_hbm(value) for value in (assignment, gradient, left_prev[0, 0], right_prev[0, 0])))
    update, left_root, right_root, left_stat, right_stat = pl.pallas_call(
        deliver,
        out_shape=results,
        in_specs=[any_space] * 7,
        out_specs=(pl.BlockSpec(memory_space=pltpu.HBM),) * 5,
        scratch_shapes=[
            pieces_vmem,
            pltpu.VMEM((8, 128), jnp.float32),
            pltpu.SMEM((1, blocks), jnp.int32),
            pltpu.SemaphoreType.DMA((6,)),
            pltpu.SemaphoreType.DMA((17,)),
        ],
        compiler_params=pltpu.CompilerParams(vmem_limit_bytes=4 * 2**20),
        name="deliver",
    )(in_hbm(assignment), *made)
    return update, left_root, right_root, left_stat[None, None], right_stat[None, None]


def solution(mesh):
    by_rows = P("pre", "train", None)
    by_owner = P("pre", "train", None, None)
    return jax.shard_map(
        shards,
        mesh=mesh,
        in_specs=(by_rows, P("pre", None), by_owner, by_owner),
        out_specs=(by_rows, by_rows, by_rows, by_owner, by_owner),
        check_vma=False,
    )
```

time: 255 us -> 105 us (0.41)
  blocking collectives: 184 us -> 0 us
  Pallas kernels: 0 us -> 105 us
  matrix products: 44.1 us -> 0 us
  local copies, waits for them, and re-layouts: 14.8 us -> 0 us
  starting transfers between devices: 4.99 us -> 0 us
  between operations: 3.7 us -> 0.64 us
  other arithmetic: 2.88 us -> 0 us
    all_to_all x3 -> x0, blocking collectives: 105 us -> none  [the longest x1 39.2 us: shards(): lax.all_to_all(outgoing, 'train', split_axis=0, concat_axis=2, tiled=True)]
    pallas_call x0 -> x2, Pallas kernels: none -> 105 us  [the longest x1 102 us: shards(): pl.pallas_call(body, out_shape=results + (jax.ShapeDtypeStruct((8, 128),...]
    psum x1 -> x0, blocking collectives: 78.8 us -> none  [shards(): lax.psum((jnp.sum(owned * owned), prec_local), ('train', 'pre'))]
    dot_general x16 -> x0, matrix products: 44.1 us -> none  [the longest x12 31.3 us: half_product(): return jnp.dot(left, right, preferred_element_type=jnp.float32)]
    scatter x3 -> x0, local copies, waits for them, and re-layouts: 10.4 us -> none  [to_blocks(): return jnp.zeros_like(in_slots).at[block_order].set(in_slots)]
    all_to_all x1 -> x0, starting transfers between devices: 4.99 us -> none  [shards(): lax.all_to_all(split_rows(left_factor), 'train', split_axis=1, concat_axi...]
  transfers between devices with their start and end apart: 1 -> 0, of which waited for: 0 -> 0; matrix products, arithmetic and copies ran while one was open for 5% -> 0% of each run, Pallas kernels for 0% -> 0%
where the time goes in v1:
time: 105 us
  Pallas kernels  105 us (100%)
    pallas_call x1, Pallas kernels, shards(): pl.pallas_call(body, out_shape=results + (jax.ShapeDtypeStruct((8, 128),...  102 us
    pallas_call x1, Pallas kernels, shards(): pl.pallas_call(deliver, out_shape=results, in_specs=[any_space] * 7, out_...  2.57 us

profile of v1, /device:TPU:1, one launch (start us, length us, event | category | flops | bytes accessed | tf_op | source)
XLA Modules:
  0.0 105.1 jit_solution(5748925914771174561)
XLA Ops:
  0.6 101.9 %shampoo.1 = (f32[32,16,512]{2,1,0:T(8,128)S(1)}, f32[32,16,512]{2,1,0:T(8,128)S(1)}, f32[32,16,512]{2,1,0:T(8,128)S(1)}, f32[512,512]{1,0:T(8,128)S(1)}, f32[512,512]{1,0:T(8,128)S(1)}, /*index=5*/f32[8,128]{1,0:T(8,128)S(1)}) custom-call(s32[1,32]{1,0:T(1,128)} %order_hbm.3, f32[32,16,512]{2,1,0:T(8,128)} %grad_hbm.1, f32[512,512]{1,0:T(8,128)} %bitcast.4, ...), custom_call_target="tpu_custom_call" | custom-call | flops 7516192768 | bytes 8388608 | tf_op jit(solution)/shard_map/shampoo/pallas_call | solution.py:441
  102.6 2.6 %deliver.1 = (f32[32,16,512]{2,1,0:T(8,128)}, f32[32,16,512]{2,1,0:T(8,128)}, f32[32,16,512]{2,1,0:T(8,128)}, f32[512,512]{1,0:T(8,128)}, f32[512,512]{1,0:T(8,128)}) custom-call(s32[1,32]{1,0:T(1,128)} %order_hbm.3, f32[32,16,512]{2,1,0:T(8,128)S(1)} %get-tuple-element.16.precond_hbm, f32[32,16,512]{2,1,0:T(8,128)S(1)} %get-tuple-element.17.left, ...), custom_call_target="tpu_custom_call" | custom-call | tf_op jit(solution)/shard_map/deliver/pallas_call | solution.py:482

commit v2 on v1

--- a/solution.py
+++ b/solution.py
@@ -10,6 +10,7 @@
 ITERS = 3
 RINGS = 8
 SUBS = 4
+PAIRS = 4
 
 
 def split(values):
@@ -95,15 +96,18 @@
     order_hbm, grad_hbm, left_prev, right_prev,
     precond_in, left_root_hbm, right_root_hbm, left_stat_hbm, right_stat_hbm, norm_hbm,
     grad, outgoing, owned, left_old, right_old, left_new, right_new,
-    left, right, precond, left_in, right_in, ready,
+    left, right, precond, left_in, right_in, ready, turned, crossed,
     high, low, other_high, other_low, factor, square, fourth, iterate, root,
     norm, norm_group, norm_all, norm_pre, norm_train, order, place,
-    in_sems, out_sems, send_sems, recv_grad, recv_sems, norm_send, norm_recv,
+    in_sems, out_sems, send_sems, recv_grad, recv_sems,
+    cross_send, cross_recv, norm_send, norm_recv,
 ):
     me, group = lax.axis_index("train"), lax.axis_index("pre")
     n, groups = lax.axis_size("train"), lax.axis_size("pre")
     blocks, rows, width = grad.shape
     plane, y_at, core_at = me // SUBS, (me // 2) % 2, me % 2
+    pair, upper_plane, peers = plane // 2, plane % 2, n // PAIRS
+    tile = width // PAIRS
 
     barrier = pltpu.get_barrier_semaphore()
 
@@ -162,14 +166,9 @@
             device_id_type=MESH,
         ).start()
 
-    def send_grad(core, half, some=None):
+    def send_grad(core, half):
         def send(j, _):
-            if some is None:
-                step, across = half * (RINGS // 2) + j // 2, (j + 1) % 2
-            else:
-                step = half * (RINGS // 2) + j
-                across = (plane + (RINGS - step) // 2 + y_at + some) % 2
-            sub = 2 * across + (core_at + core) % 2
+            step, sub = half * (RINGS // 2) + j // 2, 2 * ((j + 1) % 2) + (core_at + core) % 2
             slot = (sub - step + 10) % SUBS * SUBS + step % (RINGS // 2)
             dz, _ = offset(half, slot, core_at)
             other = device_at(dz, sub)
@@ -177,11 +176,7 @@
             push(outgoing.at[other], owned.at[at], send_sems.at[0], recv_grad.at[half], other)
             return 0
 
-        own = core_at == core
-        if some is not None:
-            own &= (plane + y_at) % 2 == some
-        count = RINGS if some is None else RINGS // 2
-        lax.fori_loop(0, count - half * jnp.where(own, 1, 0), send, 0)
+        lax.fori_loop(0, RINGS - half * jnp.where(core_at == core, 1, 0), send, 0)
 
     def send_half(source, target, which, half):
         def send(k, _):
@@ -191,17 +186,73 @@
 
         lax.fori_loop(0, n // 2 - half, send, 0)
 
-    def send_all(source, target, which):
-        send_half(source, target, which, 0)
-        send_half(source, target, which, 1)
+    def columns(which_pair):
+        return pl.ds(pl.multiple_of(which_pair % PAIRS * tile, tile), tile)
+
+    def send_root(source, target, which):
+        send_sem, recv_sem = send_sems.at[which], recv_sems.at[which]
+
+        def send_tiles(k, _):
+            place = k // (PAIRS - 1)
+            other = (pair + 2) % PAIRS * peers + place
+            skipped = pair + 1 + 2 * (place // SUBS)
+            at = columns(skipped + 1 + k % (PAIRS - 1))
+            push(source.at[other, :, at], target.at[me, :, at], send_sem, recv_sem, other)
+            return 0
+
+        def send(k, _):
+            step = k % 6
+            dz = (6 - step) // 2 * (1 - 2 * (step % 2)) * (1 - 2 * upper_plane)
+            other = device_at(dz, (step + k // 6) % SUBS)
+            push(source.at[other], target.at[me], send_sem, recv_sem, other)
+            return 0
+
+        lax.fori_loop(0, peers * (PAIRS - 1), send_tiles, 0)
+        lax.fori_loop(0, n - peers - 1, send, 0)
+        target[me] = source[me]
+
+    root_chunks = n - peers - 1 + peers * (PAIRS - 1) // PAIRS
+
+    def exchange(target, which):
+        for way in range(2):
+            to = (pair + 1 + 2 * way) % PAIRS
+            owners = (to + 2) % PAIRS * peers
+            held = target[pl.ds(owners, peers), :, columns(to)].reshape(peers * rows, tile)
+            part = held.T[way * SUBS * rows : (way + 1) * SUBS * rows]
+            turned[which, way] = part.reshape(SUBS, rows, tile)
+
+            def send(k, _):
+                other = to * peers + way * SUBS + k
+                push(
+                    turned.at[which, way, k], crossed.at[which, me % peers],
+                    cross_send.at[which], cross_recv.at[which], other,
+                )
+                return 0
+
+            lax.fori_loop(0, SUBS, send, 0)
+
+    def place_crossed(target, which):
+        arrived = crossed.at[which]
+        pltpu.make_async_copy(arrived, arrived, cross_recv.at[which]).wait()
+        at = columns(pair + 3 + 2 * upper_plane)
+        owners = (pair + 2) % PAIRS * peers
+        lane = lax.broadcasted_iota(jnp.int32, (rows, tile), 1) // rows
+        pieces = [crossed[which, sender] for sender in range(peers)]
+        for block in range(peers):
+            values = jnp.zeros((rows, tile), jnp.float32)
+            for sender in range(peers):
+                shift = (sender - block) % peers * rows
+                moved = pltpu.roll(pieces[sender], shift, 1) if shift else pieces[sender]
+                values = jnp.where(lane == sender, moved, values)
+            target[owners + block, :, at] = values
 
     def wait_bytes(ref, sem, count=n - 1):
         some = ref.at[pl.ds(0, count)]
         pltpu.make_async_copy(some, some, sem).wait()
 
-    for core, some in ((0, None), (1, 0), (1, 1)):
+    for core in range(2):
         for half in range(2):
-            send_grad(core, half, some)
+            send_grad(core, half)
     owned[n - 1] = outgoing[me]
 
     def invert(block, _):
@@ -253,8 +304,7 @@
     store_right_stat = pltpu.make_async_copy(right_new, right_stat_hbm, out_sems.at[1])
     store_right_stat.start()
     put_root(right_new, squares, right)
-    send_all(right, right_in, 1)
-    right_in[me] = right[me]
+    send_root(right, right_in, 1)
 
     def place_rows(k, _):
         half, slot = k // (n // 2), k % (n // 2)
@@ -276,7 +326,6 @@
     store_left_stat = pltpu.make_async_copy(left_new, left_stat_hbm, out_sems.at[0])
     store_left_stat.start()
     put_root(left_new, squares, left)
-    left_in[me] = left[me]
 
     def keep_split(part, values):
         right_old[:, part] = values
@@ -316,7 +365,7 @@
     def _():
         share(norm, norm_train.at[me], 0, {"train": 0})
 
-    send_all(left, left_in, 2)
+    send_root(left, left_in, 2)
 
     @pl.when(me == 0)
     def _():
@@ -326,6 +375,8 @@
         lax.fori_loop(1, groups, share_pre, 0)
         norm_pre[group] = norm_group[...]
 
+    wait_bytes(right_in, recv_sems.at[1], root_chunks)
+    exchange(right_in, 0)
     send_half(precond, precond_in, 3, 0)
 
     @pl.when(me == 0)
@@ -335,6 +386,8 @@
         norm_all[...] = jnp.sum(norm_pre[...], axis=0)
         lax.fori_loop(1, n, share_train, 0)
 
+    wait_bytes(left_in, recv_sems.at[2], root_chunks)
+    exchange(left_in, 1)
     send_half(precond, precond_in, 3, 1)
     keep_own = pltpu.make_async_copy(precond.at[me], precond_in.at[me], out_sems.at[4])
     keep_own.start()
@@ -349,9 +402,9 @@
         store.start()
         return store
 
-    wait_bytes(right_in, recv_sems.at[1])
+    place_crossed(right_in, 0)
     store_right = to_blocks(right_in, right_root_hbm, 1)
-    wait_bytes(left_in, recv_sems.at[2])
+    place_crossed(left_in, 1)
     store_left = to_blocks(left_in, left_root_hbm, 0)
 
     @pl.when(me != 0)
@@ -366,8 +419,10 @@
     store_norm = pltpu.make_async_copy(norm_all, norm_hbm, out_sems.at[5])
     store_norm.start()
     wait_bytes(owned, send_sems.at[0])
-    wait_bytes(right, send_sems.at[1])
-    wait_bytes(left, send_sems.at[2])
+    wait_bytes(right, send_sems.at[1], root_chunks)
+    wait_bytes(left, send_sems.at[2], root_chunks)
+    for which in range(2):
+        pltpu.make_async_copy(turned.at[which], turned.at[which], cross_send.at[which]).wait()
     wait_bytes(precond, send_sems.at[3])
     store_left_stat.wait()
     store_right_stat.wait()
@@ -448,6 +503,8 @@
         + [pieces_vmem] * 5
         + [
             pltpu.VMEM((2,) + pieces.shape, jnp.float32),
+            pltpu.VMEM((2, 2, SUBS, rows, width // PAIRS), jnp.float32),
+            pltpu.VMEM((2, n // PAIRS, rows, width // PAIRS), jnp.float32),
         ]
         + [square_half] * 4
         + [
@@ -468,6 +525,8 @@
             pltpu.SemaphoreType.DMA((4,)),
             pltpu.SemaphoreType.DMA((2,)),
             pltpu.SemaphoreType.DMA((4,)),
+            pltpu.SemaphoreType.DMA((2,)),
+            pltpu.SemaphoreType.DMA((2,)),
             pltpu.SemaphoreType.DMA((3,)),
             pltpu.SemaphoreType.DMA((3,)),
         ],

time: 105 us -> 102 us (0.971)
  Pallas kernels: 105 us -> 102 us
    pallas_call x1, Pallas kernels: 102 us -> 99.2 us  [shards(): pl.pallas_call(body, out_shape=results + (jax.ShapeDtypeStruct((8, 128),...]
where the time goes in v2:
time: 102 us
  Pallas kernels  102 us (100%)
    pallas_call x1, Pallas kernels, shards(): pl.pallas_call(body, out_shape=results + (jax.ShapeDtypeStruct((8, 128),...  99.2 us
    pallas_call x1, Pallas kernels, shards(): pl.pallas_call(deliver, out_shape=results, in_specs=[any_space] * 7, out_...  2.57 us

profile of v2, /device:TPU:1, one launch (start us, length us, event | category | flops | bytes accessed | tf_op | source)
XLA Modules:
  0.0 102.4 jit_solution(427728036543893454)
XLA Ops:
  0.6 99.2 %shampoo.1 = (f32[32,16,512]{2,1,0:T(8,128)S(1)}, f32[32,16,512]{2,1,0:T(8,128)S(1)}, f32[32,16,512]{2,1,0:T(8,128)S(1)}, f32[512,512]{1,0:T(8,128)S(1)}, f32[512,512]{1,0:T(8,128)S(1)}, /*index=5*/f32[8,128]{1,0:T(8,128)S(1)}) custom-call(s32[1,32]{1,0:T(1,128)} %order_hbm.3, f32[32,16,512]{2,1,0:T(8,128)} %grad_hbm.1, f32[512,512]{1,0:T(8,128)} %bitcast.4, ...), custom_call_target="tpu_custom_call" | custom-call | flops 7516192768 | bytes 8388608 | tf_op jit(solution)/shard_map/shampoo/pallas_call | solution.py:496
  99.8 2.6 %deliver.1 = (f32[32,16,512]{2,1,0:T(8,128)}, f32[32,16,512]{2,1,0:T(8,128)}, f32[32,16,512]{2,1,0:T(8,128)}, f32[512,512]{1,0:T(8,128)}, f32[512,512]{1,0:T(8,128)}) custom-call(s32[1,32]{1,0:T(1,128)} %order_hbm.3, f32[32,16,512]{2,1,0:T(8,128)S(1)} %get-tuple-element.16.precond_hbm, f32[32,16,512]{2,1,0:T(8,128)S(1)} %get-tuple-element.17.left, ...), custom_call_target="tpu_custom_call" | custom-call | tf_op jit(solution)/shard_map/deliver/pallas_call | solution.py:541

commit v3 on v2

--- a/solution.py
+++ b/solution.py
@@ -1,3 +1,5 @@
+import functools
+
 import jax
 import jax.numpy as jnp
 from jax import lax
@@ -147,10 +149,8 @@
     lax.fori_loop(0, n, pick, 0)
     pl.semaphore_wait(barrier, n - 1 + jnp.where(me == 0, groups - 1, 0))
 
-    def offset(half, k, core):
-        step = half * (RINGS // 2) + k % (RINGS // 2)
-        way = (2 * (step % 2) - 1) * (1 - 2 * core)
-        return (RINGS - step) // 2 * way, (step + k // (RINGS // 2) + 2) % SUBS
+    def away(step, core):
+        return (RINGS - step) // 2 * (2 * (step % 2) - 1) * (1 - 2 * core)
 
     def device_at(dz, sub):
         z = (plane + dz + RINGS) % RINGS
@@ -166,25 +166,29 @@
             device_id_type=MESH,
         ).start()
 
-    def send_grad(core, half):
-        def send(j, _):
-            step, sub = half * (RINGS // 2) + j // 2, 2 * ((j + 1) % 2) + (core_at + core) % 2
-            slot = (sub - step + 10) % SUBS * SUBS + step % (RINGS // 2)
-            dz, _ = offset(half, slot, core_at)
-            other = device_at(dz, sub)
-            at = half * (n // 2) + slot
+    def send_grad(core, half, step):
+        across = (half + step) % 2
+        other_core = (core_at + core) % 2
+        other = device_at(away(step, core_at), 2 * across + other_core)
+        at = half * (n // 2) + 2 * step + 1 - other_core
+
+        @pl.when(other != me)
+        def _():
             push(outgoing.at[other], owned.at[at], send_sems.at[0], recv_grad.at[half], other)
-            return 0
-
-        lax.fori_loop(0, RINGS - half * jnp.where(core_at == core, 1, 0), send, 0)
-
-    def send_half(source, target, which, half):
+
+    def grad_sender(slot):
+        half, step, other_core = slot // (n // 2), slot % (n // 2) // 2, 1 - slot % 2
+        dz = away(step, (core_at + other_core) % 2)
+        return device_at(-dz, 2 * ((half + step) % 2) + other_core)
+
+    def send_part(source, target, which, first, last):
         def send(k, _):
-            other = device_at(*offset(half, k, core_at))
+            step = k % RINGS
+            other = device_at(away(step, core_at), (step + k // RINGS + 2) % SUBS)
             push(source.at[other], target.at[me], send_sems.at[which], recv_sems.at[which], other)
             return 0
 
-        lax.fori_loop(0, n // 2 - half, send, 0)
+        lax.fori_loop(first, last, send, 0)
 
     def columns(which_pair):
         return pl.ds(pl.multiple_of(which_pair % PAIRS * tile, tile), tile)
@@ -192,23 +196,23 @@
     def send_root(source, target, which):
         send_sem, recv_sem = send_sems.at[which], recv_sems.at[which]
 
-        def send_tiles(k, _):
+        def send_tile(k):
             place = k // (PAIRS - 1)
             other = (pair + 2) % PAIRS * peers + place
             skipped = pair + 1 + 2 * (place // SUBS)
             at = columns(skipped + 1 + k % (PAIRS - 1))
             push(source.at[other, :, at], target.at[me, :, at], send_sem, recv_sem, other)
-            return 0
 
         def send(k, _):
+            send_tile(k)
             step = k % 6
             dz = (6 - step) // 2 * (1 - 2 * (step % 2)) * (1 - 2 * upper_plane)
             other = device_at(dz, (step + k // 6) % SUBS)
             push(source.at[other], target.at[me], send_sem, recv_sem, other)
             return 0
 
-        lax.fori_loop(0, peers * (PAIRS - 1), send_tiles, 0)
         lax.fori_loop(0, n - peers - 1, send, 0)
+        send_tile(n - peers - 1)
         target[me] = source[me]
 
     root_chunks = n - peers - 1 + peers * (PAIRS - 1) // PAIRS
@@ -250,9 +254,21 @@
         some = ref.at[pl.ds(0, count)]
         pltpu.make_async_copy(some, some, sem).wait()
 
-    for core in range(2):
-        for half in range(2):
-            send_grad(core, half)
+    def send_mixed(half, first, k, _):
+        for step in range(4):
+            send_grad(0, half, 4 * k + step)
+        send_grad(1, 0, first + k)
+        return 0
+
+    lax.fori_loop(0, 2, functools.partial(send_mixed, 0, 0), 0)
+    lax.fori_loop(0, 2, functools.partial(send_mixed, 1, 2), 0)
+    for half, first in ((0, 4), (1, 0)):
+
+        def send_rest(step, _):
+            send_grad(1, half, step)
+            return 0
+
+        lax.fori_loop(first, RINGS, send_rest, 0)
     owned[n - 1] = outgoing[me]
 
     def invert(block, _):
@@ -307,10 +323,7 @@
     send_root(right, right_in, 1)
 
     def place_rows(k, _):
-        half, slot = k // (n // 2), k % (n // 2)
-        _, sub = offset(half, slot, 0)
-        dz, _ = offset(half, slot, (core_at + sub) % 2)
-        at = pl.ds(pl.multiple_of(device_at(-dz, sub) * rows, rows), rows)
+        at = pl.ds(pl.multiple_of(grad_sender(k) * rows, rows), rows)
         high[at], low[at] = split(owned[k])
         return 0
 
@@ -377,7 +390,7 @@
 
     wait_bytes(right_in, recv_sems.at[1], root_chunks)
     exchange(right_in, 0)
-    send_half(precond, precond_in, 3, 0)
+    send_part(precond, precond_in, 3, 0, n * 11 // 16)
 
     @pl.when(me == 0)
     def _():
@@ -388,7 +401,7 @@
 
     wait_bytes(left_in, recv_sems.at[2], root_chunks)
     exchange(left_in, 1)
-    send_half(precond, precond_in, 3, 1)
+    send_part(precond, precond_in, 3, n * 11 // 16, n - 1)
     keep_own = pltpu.make_async_copy(precond.at[me], precond_in.at[me], out_sems.at[4])
     keep_own.start()
 

time: 102 us -> 103 us (level); the launches traced: 102 us -> 102 us
  no operation moved by 1% of the time
where the time goes in v3:
time: 103 us; the launch traced here: 102 us
  Pallas kernels  102 us (99%)
    pallas_call x1, Pallas kernels, shards(): pl.pallas_call(body, out_shape=results + (jax.ShapeDtypeStruct((8, 128),...  99.1 us
    pallas_call x1, Pallas kernels, shards(): pl.pallas_call(deliver, out_shape=results, in_specs=[any_space] * 7, out_...  2.57 us

profile of v3, /device:TPU:1, one launch (start us, length us, event | category | flops | bytes accessed | tf_op | source)
XLA Modules:
  0.0 102.3 jit_solution(6494753692350050420)
XLA Ops:
  0.6 99.1 %shampoo.1 = (f32[32,16,512]{2,1,0:T(8,128)S(1)}, f32[32,16,512]{2,1,0:T(8,128)S(1)}, f32[32,16,512]{2,1,0:T(8,128)S(1)}, f32[512,512]{1,0:T(8,128)S(1)}, f32[512,512]{1,0:T(8,128)S(1)}, /*index=5*/f32[8,128]{1,0:T(8,128)S(1)}) custom-call(s32[1,32]{1,0:T(1,128)} %order_hbm.3, f32[32,16,512]{2,1,0:T(8,128)} %grad_hbm.1, f32[512,512]{1,0:T(8,128)} %bitcast.4, ...), custom_call_target="tpu_custom_call" | custom-call | flops 7516192768 | bytes 8388608 | tf_op jit(solution)/shard_map/shampoo/pallas_call | solution.py:509
  99.8 2.6 %deliver.1 = (f32[32,16,512]{2,1,0:T(8,128)}, f32[32,16,512]{2,1,0:T(8,128)}, f32[32,16,512]{2,1,0:T(8,128)}, f32[512,512]{1,0:T(8,128)}, f32[512,512]{1,0:T(8,128)}) custom-call(s32[1,32]{1,0:T(1,128)} %order_hbm.3, f32[32,16,512]{2,1,0:T(8,128)S(1)} %get-tuple-element.16.precond_hbm, f32[32,16,512]{2,1,0:T(8,128)S(1)} %get-tuple-element.17.left, ...), custom_call_target="tpu_custom_call" | custom-call | tf_op jit(solution)/shard_map/deliver/pallas_call | solution.py:554

commit v4 on v3

--- a/solution.py
+++ b/solution.py
@@ -98,7 +98,7 @@
     order_hbm, grad_hbm, left_prev, right_prev,
     precond_in, left_root_hbm, right_root_hbm, left_stat_hbm, right_stat_hbm, norm_hbm,
     grad, outgoing, owned, left_old, right_old, left_new, right_new,
-    left, right, precond, left_in, right_in, ready, turned, crossed,
+    left, right, precond, left_in, right_in, ready, packed, packed_in, turned, crossed, doubled,
     high, low, other_high, other_low, factor, square, fourth, iterate, root,
     norm, norm_group, norm_all, norm_pre, norm_train, order, place,
     in_sems, out_sems, send_sems, recv_grad, recv_sems,
@@ -191,64 +191,119 @@
         lax.fori_loop(first, last, send, 0)
 
     def columns(which_pair):
-        return pl.ds(pl.multiple_of(which_pair % PAIRS * tile, tile), tile)
+        return pl.ds(pl.multiple_of(lax.rem(which_pair, PAIRS) * tile, tile), tile)
+
+    sign = 1 - 2 * upper_plane
+    span = SUBS * rows
+
+    def lanes(count, size):
+        return lax.broadcasted_iota(jnp.int32, (count, tile), 1) // size
 
     def send_root(source, target, which):
         send_sem, recv_sem = send_sems.at[which], recv_sems.at[which]
-
-        def send_tile(k):
-            place = k // (PAIRS - 1)
-            other = (pair + 2) % PAIRS * peers + place
-            skipped = pair + 1 + 2 * (place // SUBS)
-            at = columns(skipped + 1 + k % (PAIRS - 1))
-            push(source.at[other, :, at], target.at[me, :, at], send_sem, recv_sem, other)
+        opposite = (plane + RINGS // 2) % RINGS * SUBS
+        for place in range(SUBS):
+            ours = source[opposite + place, :, columns(pair)]
+            theirs = pltpu.roll(source[opposite + place, :, columns(pair + 2)], span, 1)
+            packed[which - 1, place] = jnp.where(lanes(rows, span) == upper_plane, ours, theirs)
 
         def send(k, _):
-            send_tile(k)
             step = k % 6
-            dz = (6 - step) // 2 * (1 - 2 * (step % 2)) * (1 - 2 * upper_plane)
+            dz = (6 - step) // 2 * (1 - 2 * (step % 2)) * sign
             other = device_at(dz, (step + k // 6) % SUBS)
             push(source.at[other], target.at[me], send_sem, recv_sem, other)
             return 0
 
-        lax.fori_loop(0, n - peers - 1, send, 0)
-        send_tile(n - peers - 1)
+        def send_packed(place, _):
+            mine = me % SUBS
+            push(
+                packed.at[which - 1, place], packed_in.at[which - 1, mine],
+                send_sem, recv_sem, opposite + place,
+            )
+            return 0
+
+        def send_both(k, _):
+            other = (plane - 3 * sign + RINGS) % RINGS * SUBS + k // (PAIRS - 1)
+            at = columns(pair + PAIRS + 2 * upper_plane + k % (PAIRS - 1))
+            push(source.at[other, :, at], target.at[me, :, at], send_sem, recv_sem, other)
+            return send(k, 0)
+
+        tiles = SUBS * (PAIRS - 1)
+        lax.fori_loop(0, tiles, send_both, 0)
+        lax.fori_loop(0, SUBS, send_packed, 0)
+        lax.fori_loop(tiles, n - peers - 1, send, 0)
         target[me] = source[me]
 
-    root_chunks = n - peers - 1 + peers * (PAIRS - 1) // PAIRS
+    root_chunks = n - peers - 1 + SUBS
+
+    ring = (3, -3, 2, -2, 1, -1)
+
+    def wrapped(z):
+        return lax.rem(z + RINGS, RINGS)
 
     def exchange(target, which):
-        for way in range(2):
-            to = (pair + 1 + 2 * way) % PAIRS
-            owners = (to + 2) % PAIRS * peers
-            held = target[pl.ds(owners, peers), :, columns(to)].reshape(peers * rows, tile)
-            part = held.T[way * SUBS * rows : (way + 1) * SUBS * rows]
-            turned[which, way] = part.reshape(SUBS, rows, tile)
-
-            def send(k, _):
-                other = to * peers + way * SUBS + k
+        def give(k, to, owners):
+            to, owners = wrapped(to), wrapped(owners)
+            at = columns(lax.div(to, 2))
+            held = target[pl.ds(owners * SUBS, SUBS), :, at].reshape(span, tile)
+            doubled[:span], doubled[span:] = held, held
+            both = doubled[...].T
+            part = jnp.where(lax.rem(to, 2) == 1, both[span:], both[:span])
+            part = part.reshape(SUBS, 2, rows // 2, tile)
+            first = (lanes(rows // 2, span) == 0)[None]
+            turned[which, k] = jnp.where(first, part[:, 0], part[:, 1])
+
+            def send(place, _):
                 push(
-                    turned.at[which, way, k], crossed.at[which, me % peers],
-                    cross_send.at[which], cross_recv.at[which], other,
+                    turned.at[which, k, place], crossed.at[which, k, me % SUBS],
+                    cross_send.at[which], cross_recv.at[which], to * SUBS + place,
                 )
                 return 0
 
             lax.fori_loop(0, SUBS, send, 0)
+
+        for k, dz in enumerate(ring):
+            give(k, plane + dz, plane + dz + RINGS // 2)
+        give(6, plane + 2 * sign, plane - sign)
+        give(7, plane - sign, plane + 2 * sign)
 
     def place_crossed(target, which):
         arrived = crossed.at[which]
         pltpu.make_async_copy(arrived, arrived, cross_recv.at[which]).wait()
-        at = columns(pair + 3 + 2 * upper_plane)
-        owners = (pair + 2) % PAIRS * peers
-        lane = lax.broadcasted_iota(jnp.int32, (rows, tile), 1) // rows
-        pieces = [crossed[which, sender] for sender in range(peers)]
-        for block in range(peers):
-            values = jnp.zeros((rows, tile), jnp.float32)
-            for sender in range(peers):
-                shift = (sender - block) % peers * rows
-                moved = pltpu.roll(pieces[sender], shift, 1) if shift else pieces[sender]
-                values = jnp.where(lane == sender, moved, values)
-            target[owners + block, :, at] = values
+        opposite, beside = wrapped(plane + RINGS // 2), wrapped(plane - 3 * sign)
+        missing = columns(pair + 3 + 2 * upper_plane)
+        halfway = rows // 2
+        mine = lanes(rows, span) == upper_plane
+        for block in range(SUBS):
+            target[opposite * SUBS + block] = jnp.zeros((rows, width), jnp.float32)
+            target[beside * SUBS + block, :, missing] = jnp.zeros((rows, tile), jnp.float32)
+            direct = packed_in[which, block]
+            for at, values in ((pair + 2, direct), (pair, pltpu.roll(direct, span, 1))):
+                target[opposite * SUBS + block, :, columns(at)] = jnp.where(mine, values, 0.0)
+
+        def take(k, giver, owners):
+            giver = wrapped(giver)
+            at, odd = columns(lax.div(giver, 2)), lax.rem(giver, 2)
+            pieces = [crossed[which, k, sender] for sender in range(SUBS)]
+            for block in range(SUBS):
+                where = owners * SUBS + block
+                top, bottom = target[where, :halfway, at], target[where, halfway:, at]
+                for sender in range(SUBS):
+                    shift = rows * ((sender - block) % (2 * SUBS))
+                    near, far = (
+                        pltpu.roll(pieces[sender], by, 1) if by else pieces[sender]
+                        for by in (shift, (shift + span) % tile)
+                    )
+                    here = lanes(halfway, rows) == SUBS * odd + sender
+                    top = jnp.where(here, jnp.where(odd == 1, far, near), top)
+                    bottom = jnp.where(here, jnp.where(odd == 1, near, far), bottom)
+                target[where, :halfway, at] = top
+                target[where, halfway:, at] = bottom
+
+        for k, dz in enumerate(ring):
+            take(k, plane - dz, opposite)
+        take(6, plane - 2 * sign, beside)
+        take(7, plane - sign, beside)
 
     def wait_bytes(ref, sem, count=n - 1):
         some = ref.at[pl.ds(0, count)]
@@ -390,7 +445,7 @@
 
     wait_bytes(right_in, recv_sems.at[1], root_chunks)
     exchange(right_in, 0)
-    send_part(precond, precond_in, 3, 0, n * 11 // 16)
+    send_part(precond, precond_in, 3, 0, n * 9 // 16)
 
     @pl.when(me == 0)
     def _():
@@ -401,7 +456,7 @@
 
     wait_bytes(left_in, recv_sems.at[2], root_chunks)
     exchange(left_in, 1)
-    send_part(precond, precond_in, 3, n * 11 // 16, n - 1)
+    send_part(precond, precond_in, 3, n * 9 // 16, n - 1)
     keep_own = pltpu.make_async_copy(precond.at[me], precond_in.at[me], out_sems.at[4])
     keep_own.start()
 
@@ -516,8 +571,11 @@
         + [pieces_vmem] * 5
         + [
             pltpu.VMEM((2,) + pieces.shape, jnp.float32),
-            pltpu.VMEM((2, 2, SUBS, rows, width // PAIRS), jnp.float32),
-            pltpu.VMEM((2, n // PAIRS, rows, width // PAIRS), jnp.float32),
+            pltpu.VMEM((2, SUBS, rows, width // PAIRS), jnp.float32),
+            pltpu.VMEM((2, SUBS, rows, width // PAIRS), jnp.float32),
+            pltpu.VMEM((2, 8, SUBS, rows // 2, width // PAIRS), jnp.float32),
+            pltpu.VMEM((2, 8, SUBS, rows // 2, width // PAIRS), jnp.float32),
+            pltpu.VMEM((width // PAIRS, width // PAIRS), jnp.float32),
         ]
         + [square_half] * 4
         + [

time: 103 us -> 101 us (0.981)
  Pallas kernels: 102 us -> 100 us
    pallas_call x1, Pallas kernels: 99.1 us -> 97.4 us  [shards(): pl.pallas_call(body, out_shape=results + (jax.ShapeDtypeStruct((8, 128),...]
where the time goes in v4:
time: 101 us
  Pallas kernels  100 us (99%)
    pallas_call x1, Pallas kernels, shards(): pl.pallas_call(body, out_shape=results + (jax.ShapeDtypeStruct((8, 128),...  97.4 us
    pallas_call x1, Pallas kernels, shards(): pl.pallas_call(deliver, out_shape=results, in_specs=[any_space] * 7, out_...  2.57 us

profile of v4, /device:TPU:1, one launch (start us, length us, event | category | flops | bytes accessed | tf_op | source)
XLA Modules:
  0.0 100.6 jit_solution(7680440631502733058)
XLA Ops:
  0.6 97.4 %shampoo.1 = (f32[32,16,512]{2,1,0:T(8,128)S(1)}, f32[32,16,512]{2,1,0:T(8,128)S(1)}, f32[32,16,512]{2,1,0:T(8,128)S(1)}, f32[512,512]{1,0:T(8,128)S(1)}, f32[512,512]{1,0:T(8,128)S(1)}, /*index=5*/f32[8,128]{1,0:T(8,128)S(1)}) custom-call(s32[1,32]{1,0:T(1,128)} %order_hbm.3, f32[32,16,512]{2,1,0:T(8,128)} %grad_hbm.1, f32[512,512]{1,0:T(8,128)} %bitcast.4, ...), custom_call_target="tpu_custom_call" | custom-call | flops 7516192768 | bytes 8388608 | tf_op jit(solution)/shard_map/shampoo/pallas_call | solution.py:564
  98.0 2.6 %deliver.1 = (f32[32,16,512]{2,1,0:T(8,128)}, f32[32,16,512]{2,1,0:T(8,128)}, f32[32,16,512]{2,1,0:T(8,128)}, f32[512,512]{1,0:T(8,128)}, f32[512,512]{1,0:T(8,128)}) custom-call(s32[1,32]{1,0:T(1,128)} %order_hbm.3, f32[32,16,512]{2,1,0:T(8,128)S(1)} %get-tuple-element.16.precond_hbm, f32[32,16,512]{2,1,0:T(8,128)S(1)} %get-tuple-element.17.left, ...), custom_call_target="tpu_custom_call" | custom-call | tf_op jit(solution)/shard_map/deliver/pallas_call | solution.py:612

commit v5 on v4

--- a/solution.py
+++ b/solution.py
@@ -202,39 +202,54 @@
     def send_root(source, target, which):
         send_sem, recv_sem = send_sems.at[which], recv_sems.at[which]
         opposite = (plane + RINGS // 2) % RINGS * SUBS
+        across = (plane + 3 * sign + RINGS) % RINGS * SUBS
+        next_pair = pair + PAIRS + sign
         for place in range(SUBS):
+            ours = source[across + place, :, columns(pair)]
+            theirs = source[across + place, :, columns(next_pair)]
+            packed[which - 1, SUBS + place] = jnp.where(
+                lanes(rows, span) == upper_plane, ours, theirs
+            )
             ours = source[opposite + place, :, columns(pair)]
             theirs = pltpu.roll(source[opposite + place, :, columns(pair + 2)], span, 1)
             packed[which - 1, place] = jnp.where(lanes(rows, span) == upper_plane, ours, theirs)
 
         def send(k, _):
-            step = k % 6
-            dz = (6 - step) // 2 * (1 - 2 * (step % 2)) * sign
-            other = device_at(dz, (step + k // 6) % SUBS)
+            step = k % 5
+            dz = (5 - step) // 2 * (1 - 2 * (step % 2)) * sign
+            other = device_at(dz, (step + k // 5 + 1) % SUBS)
             push(source.at[other], target.at[me], send_sem, recv_sem, other)
             return 0
 
         def send_packed(place, _):
-            mine = me % SUBS
-            push(
-                packed.at[which - 1, place], packed_in.at[which - 1, mine],
-                send_sem, recv_sem, opposite + place,
-            )
+            for kind, first in ((0, opposite), (SUBS, across)):
+                push(
+                    packed.at[which - 1, kind + place], packed_in.at[which - 1, kind + me % SUBS],
+                    send_sem, recv_sem, first + place,
+                )
             return 0
 
-        def send_both(k, _):
+        def send_tile(other, at):
+            push(source.at[other, :, at], target.at[me, :, at], send_sem, recv_sem, other)
+
+        def send_three(k, _):
             other = (plane - 3 * sign + RINGS) % RINGS * SUBS + k // (PAIRS - 1)
-            at = columns(pair + PAIRS + 2 * upper_plane + k % (PAIRS - 1))
-            push(source.at[other, :, at], target.at[me, :, at], send_sem, recv_sem, other)
+            send_tile(other, columns(pair + PAIRS + 2 * upper_plane + k % (PAIRS - 1)))
             return send(k, 0)
 
-        tiles = SUBS * (PAIRS - 1)
-        lax.fori_loop(0, tiles, send_both, 0)
+        def send_two(k, _):
+            for at in (pair + 2, next_pair + 2):
+                send_tile(across + k, columns(at))
+            return send(three + k, 0)
+
+        three = SUBS * (PAIRS - 1)
         lax.fori_loop(0, SUBS, send_packed, 0)
-        lax.fori_loop(tiles, n - peers - 1, send, 0)
+        lax.fori_loop(0, three, send_three, 0)
+        lax.fori_loop(0, SUBS, send_two, 0)
+        lax.fori_loop(three + SUBS, n - three - 1, send, 0)
         target[me] = source[me]
 
-    root_chunks = n - peers - 1 + SUBS
+    root_chunks = n - 3 * SUBS - 1 + 7 * SUBS // PAIRS
 
     ring = (3, -3, 2, -2, 1, -1)
 
@@ -266,11 +281,14 @@
             give(k, plane + dz, plane + dz + RINGS // 2)
         give(6, plane + 2 * sign, plane - sign)
         give(7, plane - sign, plane + 2 * sign)
+        give(8, plane - 2 * sign, plane + sign)
+        give(9, plane + sign, plane - 2 * sign)
 
     def place_crossed(target, which):
         arrived = crossed.at[which]
         pltpu.make_async_copy(arrived, arrived, cross_recv.at[which]).wait()
         opposite, beside = wrapped(plane + RINGS // 2), wrapped(plane - 3 * sign)
+        across = wrapped(plane + 3 * sign)
         missing = columns(pair + 3 + 2 * upper_plane)
         halfway = rows // 2
         mine = lanes(rows, span) == upper_plane
@@ -280,6 +298,10 @@
             direct = packed_in[which, block]
             for at, values in ((pair + 2, direct), (pair, pltpu.roll(direct, span, 1))):
                 target[opposite * SUBS + block, :, columns(at)] = jnp.where(mine, values, 0.0)
+            direct = packed_in[which, SUBS + block]
+            where = across * SUBS + block
+            target[where, :, columns(pair)] = jnp.where(mine, direct, 0.0)
+            target[where, :, columns(pair + PAIRS + sign)] = jnp.where(mine, 0.0, direct)
 
         def take(k, giver, owners):
             giver = wrapped(giver)
@@ -304,6 +326,8 @@
             take(k, plane - dz, opposite)
         take(6, plane - 2 * sign, beside)
         take(7, plane - sign, beside)
+        take(8, plane + 2 * sign, across)
+        take(9, plane + sign, across)
 
     def wait_bytes(ref, sem, count=n - 1):
         some = ref.at[pl.ds(0, count)]
@@ -571,10 +595,10 @@
         + [pieces_vmem] * 5
         + [
             pltpu.VMEM((2,) + pieces.shape, jnp.float32),
-            pltpu.VMEM((2, SUBS, rows, width // PAIRS), jnp.float32),
-            pltpu.VMEM((2, SUBS, rows, width // PAIRS), jnp.float32),
-            pltpu.VMEM((2, 8, SUBS, rows // 2, width // PAIRS), jnp.float32),
-            pltpu.VMEM((2, 8, SUBS, rows // 2, width // PAIRS), jnp.float32),
+            pltpu.VMEM((2, 2 * SUBS, rows, width // PAIRS), jnp.float32),
+            pltpu.VMEM((2, 2 * SUBS, rows, width // PAIRS), jnp.float32),
+            pltpu.VMEM((2, 10, SUBS, rows // 2, width // PAIRS), jnp.float32),
+            pltpu.VMEM((2, 10, SUBS, rows // 2, width // PAIRS), jnp.float32),
             pltpu.VMEM((width // PAIRS, width // PAIRS), jnp.float32),
         ]
         + [square_half] * 4

time: 101 us -> 99.2 us (0.982)
  Pallas kernels: 100 us -> 98.2 us
    pallas_call x1, Pallas kernels: 97.4 us -> 95.7 us  [shards(): pl.pallas_call(body, out_shape=results + (jax.ShapeDtypeStruct((8, 128),...]
where the time goes in v5:
time: 99.2 us; the launch traced here: 98.9 us
  Pallas kernels  98.2 us (99%)
    pallas_call x1, Pallas kernels, shards(): pl.pallas_call(body, out_shape=results + (jax.ShapeDtypeStruct((8, 128),...  95.7 us
    pallas_call x1, Pallas kernels, shards(): pl.pallas_call(deliver, out_shape=results, in_specs=[any_space] * 7, out_...  2.57 us

profile of v5, /device:TPU:1, one launch (start us, length us, event | category | flops | bytes accessed | tf_op | source)
XLA Modules:
  0.0 98.9 jit_solution(18370665640484197821)
XLA Ops:
  0.6 95.7 %shampoo.1 = (f32[32,16,512]{2,1,0:T(8,128)S(1)}, f32[32,16,512]{2,1,0:T(8,128)S(1)}, f32[32,16,512]{2,1,0:T(8,128)S(1)}, f32[512,512]{1,0:T(8,128)S(1)}, f32[512,512]{1,0:T(8,128)S(1)}, /*index=5*/f32[8,128]{1,0:T(8,128)S(1)}) custom-call(s32[1,32]{1,0:T(1,128)} %order_hbm.3, f32[32,16,512]{2,1,0:T(8,128)} %grad_hbm.1, f32[512,512]{1,0:T(8,128)} %bitcast.4, ...), custom_call_target="tpu_custom_call" | custom-call | flops 7516192768 | bytes 8388608 | tf_op jit(solution)/shard_map/shampoo/pallas_call | solution.py:588
  96.3 2.6 %deliver.1 = (f32[32,16,512]{2,1,0:T(8,128)}, f32[32,16,512]{2,1,0:T(8,128)}, f32[32,16,512]{2,1,0:T(8,128)}, f32[512,512]{1,0:T(8,128)}, f32[512,512]{1,0:T(8,128)}) custom-call(s32[1,32]{1,0:T(1,128)} %order_hbm.3, f32[32,16,512]{2,1,0:T(8,128)S(1)} %get-tuple-element.16.precond_hbm, f32[32,16,512]{2,1,0:T(8,128)S(1)} %get-tuple-element.17.left, ...), custom_call_target="tpu_custom_call" | custom-call | tf_op jit(solution)/shard_map/deliver/pallas_call | solution.py:636

commit v6 on v5

--- a/solution.py
+++ b/solution.py
@@ -469,7 +469,7 @@
 
     wait_bytes(right_in, recv_sems.at[1], root_chunks)
     exchange(right_in, 0)
-    send_part(precond, precond_in, 3, 0, n * 9 // 16)
+    send_part(precond, precond_in, 3, 0, n * 7 // 16)
 
     @pl.when(me == 0)
     def _():
@@ -480,7 +480,7 @@
 
     wait_bytes(left_in, recv_sems.at[2], root_chunks)
     exchange(left_in, 1)
-    send_part(precond, precond_in, 3, n * 9 // 16, n - 1)
+    send_part(precond, precond_in, 3, n * 7 // 16, n - 1)
     keep_own = pltpu.make_async_copy(precond.at[me], precond_in.at[me], out_sems.at[4])
     keep_own.start()
 

time: 99.2 us -> 99.2 us (level)
  no operation moved by 1% of the time
where the time goes in v6:
time: 99.2 us; the launch traced here: 98.9 us
  Pallas kernels  98.2 us (99%)
    pallas_call x1, Pallas kernels, shards(): pl.pallas_call(body, out_shape=results + (jax.ShapeDtypeStruct((8, 128),...  95.7 us
    pallas_call x1, Pallas kernels, shards(): pl.pallas_call(deliver, out_shape=results, in_specs=[any_space] * 7, out_...  2.57 us

profile of v6, /device:TPU:1, one launch (start us, length us, event | category | flops | bytes accessed | tf_op | source)
XLA Modules:
  0.0 98.9 jit_solution(10201970477708905644)
XLA Ops:
  0.6 95.7 %shampoo.1 = (f32[32,16,512]{2,1,0:T(8,128)S(1)}, f32[32,16,512]{2,1,0:T(8,128)S(1)}, f32[32,16,512]{2,1,0:T(8,128)S(1)}, f32[512,512]{1,0:T(8,128)S(1)}, f32[512,512]{1,0:T(8,128)S(1)}, /*index=5*/f32[8,128]{1,0:T(8,128)S(1)}) custom-call(s32[1,32]{1,0:T(1,128)} %order_hbm.3, f32[32,16,512]{2,1,0:T(8,128)} %grad_hbm.1, f32[512,512]{1,0:T(8,128)} %bitcast.4, ...), custom_call_target="tpu_custom_call" | custom-call | flops 7516192768 | bytes 8388608 | tf_op jit(solution)/shard_map/shampoo/pallas_call | solution.py:588
  96.3 2.6 %deliver.1 = (f32[32,16,512]{2,1,0:T(8,128)}, f32[32,16,512]{2,1,0:T(8,128)}, f32[32,16,512]{2,1,0:T(8,128)}, f32[512,512]{1,0:T(8,128)}, f32[512,512]{1,0:T(8,128)}) custom-call(s32[1,32]{1,0:T(1,128)} %order_hbm.3, f32[32,16,512]{2,1,0:T(8,128)S(1)} %get-tuple-element.16.precond_hbm, f32[32,16,512]{2,1,0:T(8,128)S(1)} %get-tuple-element.17.left, ...), custom_call_target="tpu_custom_call" | custom-call | tf_op jit(solution)/shard_map/deliver/pallas_call | solution.py:636

commit v7 on v6

--- a/solution.py
+++ b/solution.py
@@ -469,7 +469,7 @@
 
     wait_bytes(right_in, recv_sems.at[1], root_chunks)
     exchange(right_in, 0)
-    send_part(precond, precond_in, 3, 0, n * 7 // 16)
+    send_part(precond, precond_in, 3, 0, n * 11 // 16)
 
     @pl.when(me == 0)
     def _():
@@ -480,7 +480,7 @@
 
     wait_bytes(left_in, recv_sems.at[2], root_chunks)
     exchange(left_in, 1)
-    send_part(precond, precond_in, 3, n * 7 // 16, n - 1)
+    send_part(precond, precond_in, 3, n * 11 // 16, n - 1)
     keep_own = pltpu.make_async_copy(precond.at[me], precond_in.at[me], out_sems.at[4])
     keep_own.start()
 

time: 99.2 us -> 99.2 us (level)
  no operation moved by 1% of the time
where the time goes in v7:
time: 99.2 us; the launch traced here: 98.9 us
  Pallas kernels  98.2 us (99%)
    pallas_call x1, Pallas kernels, shards(): pl.pallas_call(body, out_shape=results + (jax.ShapeDtypeStruct((8, 128),...  95.7 us
    pallas_call x1, Pallas kernels, shards(): pl.pallas_call(deliver, out_shape=results, in_specs=[any_space] * 7, out_...  2.57 us

profile of v7, /device:TPU:1, one launch (start us, length us, event | category | flops | bytes accessed | tf_op | source)
XLA Modules:
  0.0 98.9 jit_solution(16609600369876177365)
XLA Ops:
  0.6 95.7 %shampoo.1 = (f32[32,16,512]{2,1,0:T(8,128)S(1)}, f32[32,16,512]{2,1,0:T(8,128)S(1)}, f32[32,16,512]{2,1,0:T(8,128)S(1)}, f32[512,512]{1,0:T(8,128)S(1)}, f32[512,512]{1,0:T(8,128)S(1)}, /*index=5*/f32[8,128]{1,0:T(8,128)S(1)}) custom-call(s32[1,32]{1,0:T(1,128)} %order_hbm.3, f32[32,16,512]{2,1,0:T(8,128)} %grad_hbm.1, f32[512,512]{1,0:T(8,128)} %bitcast.4, ...), custom_call_target="tpu_custom_call" | custom-call | flops 7516192768 | bytes 8388608 | tf_op jit(solution)/shard_map/shampoo/pallas_call | solution.py:588
  96.3 2.6 %deliver.1 = (f32[32,16,512]{2,1,0:T(8,128)}, f32[32,16,512]{2,1,0:T(8,128)}, f32[32,16,512]{2,1,0:T(8,128)}, f32[512,512]{1,0:T(8,128)}, f32[512,512]{1,0:T(8,128)}) custom-call(s32[1,32]{1,0:T(1,128)} %order_hbm.3, f32[32,16,512]{2,1,0:T(8,128)S(1)} %get-tuple-element.16.precond_hbm, f32[32,16,512]{2,1,0:T(8,128)S(1)} %get-tuple-element.17.left, ...), custom_call_target="tpu_custom_call" | custom-call | tf_op jit(solution)/shard_map/deliver/pallas_call | solution.py:636

commit v8 on v5

--- a/solution.py
+++ b/solution.py
@@ -204,6 +204,36 @@
         opposite = (plane + RINGS // 2) % RINGS * SUBS
         across = (plane + 3 * sign + RINGS) % RINGS * SUBS
         next_pair = pair + PAIRS + sign
+        def send(k, _):
+            step = k % 5
+            dz = (5 - step) // 2 * (1 - 2 * (step % 2)) * sign
+            other = device_at(dz, (step + k // 5 + 1) % SUBS)
+            push(source.at[other], target.at[me], send_sem, recv_sem, other)
+            return 0
+
+        def send_packed(place, _):
+            for kind, first in ((0, opposite), (SUBS, across)):
+                push(
+                    packed.at[which - 1, kind + place], packed_in.at[which - 1, kind + me % SUBS],
+                    send_sem, recv_sem, first + place,
+                )
+            return 0
+
+        def send_tile(other, at):
+            push(source.at[other, :, at], target.at[me, :, at], send_sem, recv_sem, other)
+
+        def send_three(k, _):
+            other = (plane - 3 * sign + RINGS) % RINGS * SUBS + k // (PAIRS - 1)
+            send_tile(other, columns(pair + PAIRS + 2 * upper_plane + k % (PAIRS - 1)))
+            return send(k, 0)
+
+        def send_two(k, _):
+            for at in (pair + 2, next_pair + 2):
+                send_tile(across + k, columns(at))
+            return send(three + k, 0)
+
+        three = SUBS * (PAIRS - 1)
+        lax.fori_loop(0, three, send_three, 0)
         for place in range(SUBS):
             ours = source[across + place, :, columns(pair)]
             theirs = source[across + place, :, columns(next_pair)]
@@ -213,38 +243,7 @@
             ours = source[opposite + place, :, columns(pair)]
             theirs = pltpu.roll(source[opposite + place, :, columns(pair + 2)], span, 1)
             packed[which - 1, place] = jnp.where(lanes(rows, span) == upper_plane, ours, theirs)
-
-        def send(k, _):
-            step = k % 5
-            dz = (5 - step) // 2 * (1 - 2 * (step % 2)) * sign
-            other = device_at(dz, (step + k // 5 + 1) % SUBS)
-            push(source.at[other], target.at[me], send_sem, recv_sem, other)
-            return 0
-
-        def send_packed(place, _):
-            for kind, first in ((0, opposite), (SUBS, across)):
-                push(
-                    packed.at[which - 1, kind + place], packed_in.at[which - 1, kind + me % SUBS],
-                    send_sem, recv_sem, first + place,
-                )
-            return 0
-
-        def send_tile(other, at):
-            push(source.at[other, :, at], target.at[me, :, at], send_sem, recv_sem, other)
-
-        def send_three(k, _):
-            other = (plane - 3 * sign + RINGS) % RINGS * SUBS + k // (PAIRS - 1)
-            send_tile(other, columns(pair + PAIRS + 2 * upper_plane + k % (PAIRS - 1)))
-            return send(k, 0)
-
-        def send_two(k, _):
-            for at in (pair + 2, next_pair + 2):
-                send_tile(across + k, columns(at))
-            return send(three + k, 0)
-
-        three = SUBS * (PAIRS - 1)
         lax.fori_loop(0, SUBS, send_packed, 0)
-        lax.fori_loop(0, three, send_three, 0)
         lax.fori_loop(0, SUBS, send_two, 0)
         lax.fori_loop(three + SUBS, n - three - 1, send, 0)
         target[me] = source[me]
@@ -555,7 +554,8 @@
     pairs = ((left, left_out), (right, right_out), (left_stat, left_stat_out), (right_stat, right_stat_out))
     stores = []
     for i, (source, target) in enumerate(pairs):
-        stores += copy_in_parts(source, target, out_sems.at[pl.ds(4 * i, 4)])
+        stores.append(pltpu.make_async_copy(source, target, out_sems.at[i]))
+        stores[-1].start()
     load_order.wait()
     load_norm.wait()
     graft = jnp.sqrt(norm[0:1, 0:1] / (norm[4:5, 0:1] + 1e-6))

time: 99.2 us -> 99.1 us (level)
  no operation moved by 1% of the time
where the time goes in v8:
time: 99.1 us; the launch traced here: 98.8 us
  Pallas kernels  98.2 us (99%)
    pallas_call x1, Pallas kernels, shards(): pl.pallas_call(body, out_shape=results + (jax.ShapeDtypeStruct((8, 128),...  95.6 us
    pallas_call x1, Pallas kernels, shards(): pl.pallas_call(deliver, out_shape=results, in_specs=[any_space] * 7, out_...  2.58 us

profile of v8, /device:TPU:1, one launch (start us, length us, event | category | flops | bytes accessed | tf_op | source)
XLA Modules:
  0.0 98.8 jit_solution(14433224391683881098)
XLA Ops:
  0.6 95.6 %shampoo.1 = (f32[32,16,512]{2,1,0:T(8,128)S(1)}, f32[32,16,512]{2,1,0:T(8,128)S(1)}, f32[32,16,512]{2,1,0:T(8,128)S(1)}, f32[512,512]{1,0:T(8,128)S(1)}, f32[512,512]{1,0:T(8,128)S(1)}, /*index=5*/f32[8,128]{1,0:T(8,128)S(1)}) custom-call(s32[1,32]{1,0:T(1,128)} %order_hbm.3, f32[32,16,512]{2,1,0:T(8,128)} %grad_hbm.1, f32[512,512]{1,0:T(8,128)} %bitcast.4, ...), custom_call_target="tpu_custom_call" | custom-call | flops 7516192768 | bytes 8388608 | tf_op jit(solution)/shard_map/shampoo/pallas_call | solution.py:588
  96.3 2.6 %deliver.1 = (f32[32,16,512]{2,1,0:T(8,128)}, f32[32,16,512]{2,1,0:T(8,128)}, f32[32,16,512]{2,1,0:T(8,128)}, f32[512,512]{1,0:T(8,128)}, f32[512,512]{1,0:T(8,128)}) custom-call(s32[1,32]{1,0:T(1,128)} %order_hbm.3, f32[32,16,512]{2,1,0:T(8,128)S(1)} %get-tuple-element.16.precond_hbm, f32[32,16,512]{2,1,0:T(8,128)S(1)} %get-tuple-element.17.left, ...), custom_call_target="tpu_custom_call" | custom-call | tf_op jit(solution)/shard_map/deliver/pallas_call | solution.py:636
